TPU v7x, 32 devices: a whole 2x2x4 slice. The times are simulated.
32 devices in a mesh: graphs: 2 (over x), dom: 16 (over z, y, core).
Axes of the slice: x: 2, y: 2, z: 4, core: 2. Of those that a mesh axis runs over, the one named last changes fastest.
Arguments:
- node_feats: float32 [4096, 256], P(('graphs', 'dom')), parts along dimension 0, may hold values from -6 to 6
- norm_gain: float32 [256], replicated, may hold values from 0.1 to 1.9
- w_query: bfloat16 [256, 256], replicated, may hold values from -32 to 32
- w_key: bfloat16 [256, 256], replicated, may hold values from -1 to 1
- w_value: bfloat16 [256, 256], replicated, may hold values from -0.375 to 0.375
- w_out: bfloat16 [256, 256], replicated, may hold values from -0.75 to 0.75
- msg_src_w: bfloat16 [256, 256], replicated, may hold values from -0.25 to 0.25
- msg_dst_w: bfloat16 [256, 256], replicated, may hold values from -0.25 to 0.25
- msg_bias: float32 [256], replicated, may hold values from -4 to 4
- msg_out_w: bfloat16 [256, 256], replicated, may hold values from -0.25 to 0.25
- msg_out_bias: float32 [256], replicated, may hold values from -3 to 3
- mlp_gain: float32 [256], replicated, may hold values from 0.1 to 1.9
- mlp_up: bfloat16 [256, 1024], replicated, may hold values from -0.375 to 0.375
- mlp_down: bfloat16 [1024, 256], replicated, may hold values from -0.1875 to 0.1875
- send_list: int32 [32, 16, 4], P(('graphs', 'dom')), parts along dimension 0, may hold values from 0 to 127
- send_count: int32 [32, 16], P('graphs', 'dom'), parts along dimension 0, may hold values from 0 to 4, as said below
- edge_src: int32 [32, 8, 128], P(('graphs', 'dom')), parts along dimension 0, may hold values from 0 to 191
- edge_dst: int32 [32, 8, 128], P(('graphs', 'dom')), parts along dimension 0, may hold values from 0 to 127
- edge_count: int32 [32], P(('graphs', 'dom')), parts along dimension 0, may hold values from 256 to 1024, as said below
Outputs:
- out_feats: float32 [4096, 256], P(('graphs', 'dom')), parts along dimension 0
There are 2 independent parts, one for each index of `graphs`. A program takes and returns all parts, laid end to end along the dimension named above; an argument that names none is the same for every part. Nothing has to cross between parts.
Inputs may be any that keep to these rules, and one draw needn't show every extreme that they name: `send_list`: entries in slots at or past the count are arbitrary local rows. `send_count`: some sender fills all 4 slots to some receiver. `edge_src`: slots below 128 are local nodes; slot 128 + p * 4 + j is slot j of the rows received from partition p. `edge_count`: live edge slots come first in a partition's order; some partition has all 1024 slots live.
All inputs are finite; a program needn't handle non-finite values.
Results may differ from a plain program's by a relative error of at most 0.0057.
Values may be sent and summed in bfloat16 or wider, within the bound.
A program may use at most 64 MiB of HBM per device.

v0:
```python
import jax
import jax.numpy as jnp
from jax import lax
from jax.sharding import PartitionSpec as P

HEADS = 8


def rms_norm(features, scale_gain):
    return (
        features
        * lax.rsqrt(jnp.mean(features * features, axis=-1, keepdims=True) + 1e-06)
        * scale_gain.astype(jnp.float32)
    )


def blocked(running, arrays, first_row, handler):
    total_rows = arrays[0].shape[0]
    block_rows = 1
    for candidate in range(min(total_rows, 1024), 0, -1):
        if total_rows % candidate == 0:
            block_rows = candidate
            break
    if block_rows == total_rows:
        return handler(running, first_row, *arrays)
    block_count = total_rows // block_rows

    def step_block(block_index, state_now):
        block_begin = block_index * block_rows
        sliced_items = tuple(
            (lax.dynamic_slice_in_dim(item, block_begin, block_rows, 0) for item in arrays)
        )
        return handler(state_now, first_row + block_begin, *sliced_items)

    return lax.fori_loop(0, block_count, step_block, running)


def body(
    node_feats,
    norm_gain,
    w_query,
    w_key,
    w_value,
    w_out,
    msg_src_w,
    msg_dst_w,
    msg_bias,
    msg_out_w,
    msg_out_bias,
    mlp_gain,
    mlp_up,
    mlp_down,
    send_list,
    send_count,
    edge_src,
    edge_dst,
    edge_count,
):
    node_rows, model_width = node_feats.shape
    head_count = HEADS
    head_size = model_width // head_count
    slot_depth = send_list.shape[2]
    normed = rms_norm(node_feats, norm_gain).astype(jnp.bfloat16)
    queries = (
        jnp.dot(normed, w_query, preferred_element_type=jnp.float32)
        .astype(jnp.bfloat16)
        .reshape(node_rows, head_count, head_size)
    )

    def attend_block(running, key_block, value_block):
        run_max, run_total, weighted_sum = running
        block_rows = key_block.shape[0]
        key_heads = key_block.reshape(block_rows, head_count, head_size)
        value_heads = value_block.reshape(block_rows, head_count, head_size)
        scores = jnp.einsum(
            "qhd,khd->hqk", queries, key_heads, preferred_element_type=jnp.float32
        ) * head_size ** (-0.5)
        new_max = jnp.maximum(run_max, jnp.max(scores, axis=-1))
        rescale = jnp.exp(run_max - new_max)
        weights = jnp.exp(scores - new_max[:, :, None])
        new_total = run_total * rescale + jnp.sum(weights, axis=-1)
        mixed = jnp.einsum(
            "hqk,khd->qhd",
            weights.astype(jnp.bfloat16),
            value_heads,
            preferred_element_type=jnp.float32,
        ).reshape(node_rows, model_width)
        column_scale = jnp.repeat(jnp.transpose(rescale), head_size, axis=1)
        return (new_max, new_total, weighted_sum * column_scale + mixed)

    def project_block(running, row_block):
        key_block = jnp.dot(row_block, w_key, preferred_element_type=jnp.float32).astype(
            jnp.bfloat16
        )
        value_block = jnp.dot(row_block, w_value, preferred_element_type=jnp.float32).astype(
            jnp.bfloat16
        )
        return attend_block(running, key_block, value_block)

    initial = (
        jnp.full((head_count, node_rows), -1e30, jnp.float32),
        jnp.zeros((head_count, node_rows), jnp.float32),
        jnp.zeros((node_rows, model_width), jnp.float32),
    )
    lists_in = lax.all_to_all(send_list[0], "dom", split_axis=0, concat_axis=0, tiled=True)
    sender_ids = jnp.arange(lists_in.shape[0], dtype=jnp.int32)
    wanted = (sender_ids[:, None] * node_rows + lists_in).reshape(-1).astype(jnp.int32)
    picked_empty = jnp.zeros((wanted.shape[0], model_width), jnp.bfloat16)

    def project_pick(running, block_start, row_block):
        attention_state, picked = running
        attention_state = project_block(attention_state, row_block)
        block_rows = row_block.shape[0]
        offset = wanted - block_start
        inside = (offset >= 0) & (offset < block_rows)
        taken_rows = row_block[jnp.clip(offset, 0, block_rows - 1)]
        picked = jnp.where(inside[:, None], taken_rows, picked)
        return (attention_state, picked)

    final_state, received_flat = blocked(
        (initial, picked_empty),
        (jax.tree.map(lambda part: lax.all_gather(part, "dom", axis=0, tiled=True), normed),),
        jnp.int32(0),
        project_pick,
    )
    final_total = jnp.repeat(jnp.transpose(final_state[1]), head_size, axis=1)
    attended = (final_state[2] / final_total).astype(jnp.bfloat16)
    global_part = jnp.dot(attended, w_out, preferred_element_type=jnp.float32)
    source_table = jnp.concatenate([normed, received_flat], axis=0)
    slot_total = source_table.shape[0]
    remote_live = (jnp.arange(slot_depth, dtype=jnp.int32)[None, :] < send_count[:, 0:1]).reshape(
        -1
    )
    slot_valid = jnp.concatenate(
        [jnp.ones((node_rows,), jnp.bfloat16), remote_live.astype(jnp.bfloat16)]
    )
    slot_ids = jnp.arange(slot_total, dtype=jnp.int32)
    node_ids = jnp.arange(node_rows, dtype=jnp.int32)
    lane_ids = jnp.arange(edge_src.shape[2], dtype=jnp.int32)
    edge_limit = edge_count[0]
    bias_first = msg_bias.astype(jnp.float32)
    bias_second = msg_out_bias.astype(jnp.float32)

    def tile_step(tile_index, aggregate):
        src_tile = lax.dynamic_index_in_dim(edge_src[0], tile_index, 0, keepdims=False)
        dst_tile = lax.dynamic_index_in_dim(edge_dst[0], tile_index, 0, keepdims=False)
        pick_src = (src_tile[:, None] == slot_ids[None, :]).astype(jnp.bfloat16)
        src_feats = jnp.dot(pick_src, source_table, preferred_element_type=jnp.float32).astype(
            jnp.bfloat16
        )
        in_range = (tile_index * edge_src.shape[2] + lane_ids < edge_limit).astype(jnp.float32)
        edge_live = jnp.dot(pick_src, slot_valid, preferred_element_type=jnp.float32) * in_range
        pick_dst = (dst_tile[:, None] == node_ids[None, :]).astype(jnp.bfloat16)
        dst_feats = jnp.dot(pick_dst, normed, preferred_element_type=jnp.float32).astype(
            jnp.bfloat16
        )
        pre_act = (
            jnp.dot(src_feats, msg_src_w, preferred_element_type=jnp.float32)
            + jnp.dot(dst_feats, msg_dst_w, preferred_element_type=jnp.float32)
            + bias_first
        )
        hidden = jax.nn.silu(pre_act).astype(jnp.bfloat16)
        message = (
            jnp.dot(hidden, msg_out_w, preferred_element_type=jnp.float32) + bias_second
        ).astype(jnp.bfloat16)
        spread = (pick_dst.astype(jnp.float32) * edge_live[:, None]).astype(jnp.bfloat16)
        return aggregate + lax.dot_general(
            spread, message, (((0,), (0,)), ((), ())), preferred_element_type=jnp.float32
        )

    tile_count = edge_src.shape[1]
    local_part = lax.fori_loop(
        0, tile_count, tile_step, jnp.zeros((node_rows, model_width), jnp.float32)
    )
    mid = node_feats + local_part + global_part
    mid_normed = rms_norm(mid, mlp_gain).astype(jnp.bfloat16)
    lifted = jax.nn.gelu(jnp.dot(mid_normed, mlp_up, preferred_element_type=jnp.float32)).astype(
        jnp.bfloat16
    )
    return mid + jnp.dot(lifted, mlp_down, preferred_element_type=jnp.float32)


def solution(mesh):
    return jax.shard_map(
        body,
        mesh=mesh,
        in_specs=(
            P(("graphs", "dom"), None),
            P(),
            P(),
            P(),
            P(),
            P(),
            P(),
            P(),
            P(),
            P(),
            P(),
            P(),
            P(),
            P(),
            P(("graphs", "dom"), None, None),
            P("graphs", "dom"),
            P(("graphs", "dom"), None, None),
            P(("graphs", "dom"), None, None),
            P(("graphs", "dom")),
        ),
        out_specs=P(("graphs", "dom"), None),
        check_vma=False,
    )
```

profile of v0, /device:TPU:0, one launch (start us, length us, event | category | flops | bytes accessed | tf_op | source)
XLA Modules:
  0.0 94.0 jit_solution(13545801613496286900)
XLA Ops:
  6.5 1.1 %multiply_reduce_fusion.1 = f32[128]{0:T(128)S(1)} fusion(f32[128,256]{1,0:T(8,128)} %param.23), kind=kLoop, calls=%fused_computation.70 | loop fusion | flops 65408 | bytes 131584 | tf_op jit(solution)/shard_map/reduce_sum | solution.py:12
  7.6 1.6 %multiply_convert_fusion.4 = bf16[128,256]{1,0:T(8,128)(2,1)} fusion(f32[128,256]{1,0:T(8,128)} %param.23, f32[256]{0:T(256)} %param.24, f32[128]{0:T(128)S(1)} %add_rsqrt_fusion.1), kind=kLoop, calls=%fused_computation.69 | loop fusion | flops 98304 | bytes 198144 | tf_op jit(solution)/shard_map/convert_element_type | solution.py:63
  9.3 1.3 %copy.28 = s32[16,1,4]{2,1,0:T(1,128)} copy(s32[16,1,4]{0,2,1:T(4,128)} %bitcast.119) | data formatting | bytes 512 | tf_op jit(solution)/shard_map/all_to_all | solution.py:105
  10.6 7.4 %all-to-all-start = ((s32[16,1,4]{2,1,0:T(1,128)}), s32[16,1,4]{2,1,0:T(1,128)S(1)}, u32[]{:S(2)}, u32[]{:S(2)}) async-start(s32[16,1,4]{2,1,0:T(1,128)} %copy.28), calls=%async_computation | async-start | bytes 16384 | tf_op jit(solution)/shard_map/all_to_all | solution.py:105
  18.9 1.1 %convolution_convert_fusion.4 = bf16[128,256]{1,0:T(8,128)(2,1)S(1)} fusion(bf16[128,256]{1,0:T(8,128)(2,1)} %multiply_convert_fusion.4, bf16[256,256]{1,0:T(8,128)(2,1)} %param.25), kind=kOutput, calls=%fused_computation.51 | convolution fusion | flops 16809984 | bytes 262144 | tf_op jit(solution)/shard_map/dot_general | solution.py:65
  20.3 4.1 %all-to-all-done = s32[16,1,4]{2,1,0:T(1,128)S(1)} async-done(((s32[16,1,4]{2,1,0:T(1,128)}), s32[16,1,4]{2,1,0:T(1,128)S(1)}, u32[]{:S(2)}, u32[]{:S(2)}) %all-to-all-start) | async-done | bytes 288 | tf_op jit(solution)/shard_map/all_to_all | solution.py:105
  25.8 24.5 %all-gather.2.cloned.1.call-done = bf16[2048,256]{1,0:T(8,128)(2,1)} async-done(((bf16[128,256]{1,0:T(8,128)(2,1)}), bf16[2048,256]{1,0:T(8,128)(2,1)}) %all-gather.2.cloned.1.call-update) | async-done | bytes 1048592 | tf_op jit(solution)/shard_map/all_gather | solution.py:122
  50.3 13.8 %while.36 = (s32[]{:T(128)}, f32[8,128]{1,0:T(8,128)S(1)}, f32[8,128]{1,0:T(8,128)S(1)}, f32[128,256]{0,1:T(8,128)S(1)}, bf16[64,256]{1,0:T(8,128)(2,1)S(1)}, /*...) while((s32[]{:T(128)}, f32[8,128]{1,0:T(8,128)S(1)}, ...), condition=%wide.region_4.5_spmd.clone, body=%wide.region_1.4_spmd.clone.sunk | while | flops 411704896 | bytes 17864272 | solution.py:35
  50.3 1.2 %constant_dynamic-slice_fusion.2 = bf16[1024,256]{1,0:T(8,128)(2,1)S(1)} fusion(bf16[2048,256]{1,0:T(8,128)(2,1)} %get-tuple-element.827, s32[]{:T(128)S(6)} %select_n.49), kind=kLoop, calls=%fused_computation.23.clone.1 | loop fusion | bytes 1048580 | tf_op jit(solution)/shard_map/while/body/eval_jaxpr/dynamic_slice | solution.py:31
  52.3 1.2 %convolution_convert_fusion.8 = bf16[1024,256]{0,1:T(8,128)(2,1)S(1)} fusion(bf16[1024,256]{1,0:T(8,128)(2,1)S(1)} %constant_dynamic-slice_fusion.2, bf16[256,256]{1,0:T(8,128)(2,1)} %get-tuple-element.830), kind=kOutput, calls=%fused_computation.9.clone.1 | convolution fusion | flops 134479872 | bytes 1179648 | tf_op jit(solution)/shard_map/while/body/eval_jaxpr/dot_general | solution.py:95
  53.6 1.2 %convolution_convert_fusion.7 = bf16[1024,256]{0,1:T(8,128)(2,1)S(1)} fusion(bf16[1024,256]{1,0:T(8,128)(2,1)S(1)} %constant_dynamic-slice_fusion.2, bf16[256,256]{1,0:T(8,128)(2,1)} %get-tuple-element.828), kind=kOutput, calls=%fused_computation.10.clone.1 | convolution fusion | flops 134479872 | bytes 1179648 | tf_op jit(solution)/shard_map/while/body/eval_jaxpr/dot_general | solution.py:92
  57.3 1.1 %constant_dynamic-slice_fusion.2 = bf16[1024,256]{1,0:T(8,128)(2,1)S(1)} fusion(bf16[2048,256]{1,0:T(8,128)(2,1)} %get-tuple-element.827, s32[]{:T(128)S(6)} %select_n.49), kind=kLoop, calls=%fused_computation.23.clone.1 | loop fusion | bytes 1048580 | tf_op jit(solution)/shard_map/while/body/eval_jaxpr/dynamic_slice | solution.py:31
  59.2 1.2 %convolution_convert_fusion.8 = bf16[1024,256]{0,1:T(8,128)(2,1)S(1)} fusion(bf16[1024,256]{1,0:T(8,128)(2,1)S(1)} %constant_dynamic-slice_fusion.2, bf16[256,256]{1,0:T(8,128)(2,1)} %get-tuple-element.830), kind=kOutput, calls=%fused_computation.9.clone.1 | convolution fusion | flops 134479872 | bytes 1179648 | tf_op jit(solution)/shard_map/while/body/eval_jaxpr/dot_general | solution.py:95
  60.4 1.2 %convolution_convert_fusion.7 = bf16[1024,256]{0,1:T(8,128)(2,1)S(1)} fusion(bf16[1024,256]{1,0:T(8,128)(2,1)S(1)} %constant_dynamic-slice_fusion.2, bf16[256,256]{1,0:T(8,128)(2,1)} %get-tuple-element.828), kind=kOutput, calls=%fused_computation.10.clone.1 | convolution fusion | flops 134479872 | bytes 1179648 | tf_op jit(solution)/shard_map/while/body/eval_jaxpr/dot_general | solution.py:92
  64.2 21.4 %while.37 = (s32[]{:T(128)}, f32[128,256]{1,0:T(8,128)S(1)}, s32[1,8,128]{2,1,0:T(8,128)}, s32[]{:T(128)}, s32[1,8,128]{2,1,0:T(8,128)}, /*index=5*/bf16[192]{0:...) while((s32[]{:T(128)}, f32[128,256]{1,0:T(8,128)S(1)}, ...), condition=%wide.region_6.7_spmd.clone.clone, body=%wide.region_5.6_spmd.clone.clone.sunk | while | flops 80314752 | bytes 1220927 | solution.py:172
  65.0 0.8 fusion.113
  67.7 0.8 fusion.113
  70.4 0.8 fusion.113
  73.0 0.8 fusion.113
  75.7 0.8 fusion.113
  78.4 0.8 fusion.113
  81.0 0.8 fusion.113
  83.7 0.8 fusion.113
  86.0 1.1 %convolution_add_fusion.3 = f32[128,256]{1,0:T(8,128)} fusion(f32[128,256]{1,0:T(8,128)S(1)} %get-tuple-element.641, bf16[1024,256]{1,0:T(8,128)(2,1)S(1)} %copy-done, bf16[256,1024]{1,0:T(8,128)(2,1)S(1)} %copy-done.7, f32[256]{0:T(256)S(1)} %copy-done.10, f32[128]{0:T(128)S(1)} %add_rsqrt_fusion), kind=kOutput, calls=%fused_computation.49 | convolution fusion | flops 135528448 | bytes 1312256 | tf_op jit(solution)/shard_map/dot_general | solution.py:180
  (109 shorter events, 23.5 us)
Async XLA Ops:
  6.5 79.5 %copy-start = (bf16[1024,256]{1,0:T(8,128)(2,1)S(1)}, bf16[1024,256]{1,0:T(8,128)(2,1)}, u32[]{:S(2)}) copy-start(bf16[1024,256]{1,0:T(8,128)(2,1)} %param.36) | copy-start | bytes 1572868
  6.5 43.7 %all-gather.2.cloned.1.call-start = ((), (), s32[]{:S(2)}) async-start(), calls=%async_computation.1 | async-start | bytes 1114112 | tf_op jit(solution)/shard_map/all_gather | solution.py:122
  10.6 13.8 %all-to-all-start = ((s32[16,1,4]{2,1,0:T(1,128)}), s32[16,1,4]{2,1,0:T(1,128)S(1)}, u32[]{:S(2)}, u32[]{:S(2)}) async-start(s32[16,1,4]{2,1,0:T(1,128)} %copy.28), calls=%async_computation | async-start | bytes 16384 | tf_op jit(solution)/shard_map/all_to_all | solution.py:105
  50.2 13.9 %copy-start.4 = (bf16[128,256]{1,0:T(8,128)(2,1)S(1)}, bf16[128,256]{1,0:T(8,128)(2,1)}, u32[]{:S(2)}) copy-start(bf16[128,256]{1,0:T(8,128)(2,1)} %multiply_convert_fusion.4) | copy-start | bytes 196612
  50.2 13.9 %copy-start.1 = (bf16[256,256]{1,0:T(8,128)(2,1)S(1)}, bf16[256,256]{1,0:T(8,128)(2,1)}, u32[]{:S(2)}) copy-start(bf16[256,256]{1,0:T(8,128)(2,1)} %param.29) | copy-start | bytes 393220
  50.2 13.9 %copy-start.2 = (bf16[256,256]{1,0:T(8,128)(2,1)S(1)}, bf16[256,256]{1,0:T(8,128)(2,1)}, u32[]{:S(2)}) copy-start(bf16[256,256]{1,0:T(8,128)(2,1)} %param.32) | copy-start | bytes 393220
  50.2 13.9 %copy-start.6 = (f32[256]{0:T(256)S(1)}, f32[256]{0:T(256)}, u32[]{:S(2)}) copy-start(f32[256]{0:T(256)} %param.33) | copy-start | bytes 3076
  50.2 13.9 %copy-start.8 = (bf16[256,256]{1,0:T(8,128)(2,1)S(1)}, bf16[256,256]{1,0:T(8,128)(2,1)}, u32[]{:S(2)}) copy-start(bf16[256,256]{1,0:T(8,128)(2,1)} %param.30) | copy-start | bytes 393220
  50.2 13.9 %copy-start.9 = (f32[256]{0:T(256)S(1)}, f32[256]{0:T(256)}, u32[]{:S(2)}) copy-start(f32[256]{0:T(256)} %param.31) | copy-start | bytes 3076
  64.2 21.5 %copy-start.3 = (f32[128,256]{1,0:T(8,128)S(1)}, f32[128,256]{1,0:T(8,128)}, u32[]{:S(2)}) copy-start(f32[128,256]{1,0:T(8,128)} %param.23) | copy-start | bytes 393220
  64.2 21.5 %copy-start.5 = (bf16[256,256]{1,0:T(8,128)(2,1)S(1)}, bf16[256,256]{1,0:T(8,128)(2,1)}, u32[]{:S(2)}) copy-start(bf16[256,256]{1,0:T(8,128)(2,1)} %param.28) | copy-start | bytes 393220
  64.2 21.8 %copy-start.7 = (bf16[256,1024]{1,0:T(8,128)(2,1)S(1)}, bf16[256,1024]{1,0:T(8,128)(2,1)}, u32[]{:S(2)}) copy-start(bf16[256,1024]{1,0:T(8,128)(2,1)} %param.35) | copy-start | bytes 1572868
  64.2 21.8 %copy-start.10 = (f32[256]{0:T(256)S(1)}, f32[256]{0:T(256)}, u32[]{:S(2)}) copy-start(f32[256]{0:T(256)} %param.34) | copy-start | bytes 3076
Sparse Core Ops, SparseCore 0:
  9.5 40.6 all-gather.1
where the time goes:
time: 94.9 us; the launch traced here: 94 us
  waiting for transfers between devices  28.6 us (30%)
  matrix products  26.1 us (28%)
  between operations  13.7 us (14%)
  local copies, waits for them, and re-layouts  12 us (13%)
  starting transfers between devices  7.39 us (8%)
  other arithmetic  5.84 us (6%)
    all_gather x1, waiting for transfers between devices, body(): lax.all_gather(part, 'dom', axis=0, tiled=True)  24.5 us
    all_to_all x1, starting transfers between devices, body(): lax.all_to_all(send_list[0], 'dom', split_axis=0, concat_axis=0, tiled=True)  7.39 us
    dot_general x8, matrix products, tile_step(): jnp.dot(pick_src, slot_valid, preferred_element_type=jnp.float32) * in_range  6.79 us
    eq x8, local copies, waits for them, and re-layouts, tile_step(): pick_src = (src_tile[:, None] == slot_ids[None, :]).astype(jnp.bfloat16)  5.78 us
    all_to_all x1, waiting for transfers between devices, body(): lax.all_to_all(send_list[0], 'dom', split_axis=0, concat_axis=0, tiled=True)  4.12 us
    dot_general x8, matrix products, tile_step(): jnp.dot(dst_feats, msg_dst_w, preferred_element_type=jnp.float32)  2.89 us
    dot_general x8, matrix products, tile_step(): lax.dot_general(spread, message, (((0,), (0,)), ((), ())), preferred_elem...  2.88 us
    dot_general x8, matrix products, tile_step(): jnp.dot(src_feats, msg_src_w, preferred_element_type=jnp.float32)  2.78 us
  transfers between devices with their start and end apart: 2, of which 2 were waited for; matrix products, arithmetic and copies ran while one was open for 5% of the time, Pallas kernels for 0%

commit v1 on v0

v1 whole, which is shorter than its diff:
```python
import functools
import math

import jax
import jax.numpy as jnp
from jax import lax
from jax.experimental import pallas as pl
from jax.experimental.pallas import tpu as pltpu
from jax.sharding import PartitionSpec as P

HEADS = 8
MESH = pl.DeviceIdType.MESH
BF16 = jnp.bfloat16
F32 = jnp.float32


def dot(a, b, dims=((1,), (0,))):
    return lax.dot_general(a, b, (dims, ((), ())), preferred_element_type=F32)


def rms_norm(features, gain):
    return features * lax.rsqrt(jnp.mean(features * features, axis=-1, keepdims=True) + 1e-06) * gain


def kernel(
    n_dom,
    gain_ref,
    msg_bias_ref,
    msg_out_bias_ref,
    mlp_gain_ref,
    list_ref,
    count_ref,
    src_ref,
    dst_ref,
    limit_ref,
    feats_hbm,
    wq_hbm,
    wk_hbm,
    msrc_hbm,
    mdst_hbm,
    mout_hbm,
    wv_hbm,
    wo_hbm,
    up_hbm,
    down_hbm,
    out_ref,
    feats,
    wq,
    wk,
    msrc,
    mdst,
    mout,
    wv,
    wo,
    up,
    down,
    gathered,
    list_out,
    list_in,
    wanted_ref,
    qk,
    acc,
    top,
    total,
    table,
    onehot_src,
    onehot_dst,
    load_sem,
    ring_send,
    ring_recv,
    half_send,
    half_recv,
    pair_send,
    pair_recv,
    list_send,
    list_recv,
):
    rows, width = feats.shape
    depth = list_ref.shape[-1]
    slots = n_dom * depth
    lanes = table.shape[0]
    chips = n_dom // 2
    half = chips // 2
    mid_row = rows // 2
    head = width // HEADS

    sources = (feats_hbm, wq_hbm, wk_hbm, msrc_hbm, mdst_hbm, mout_hbm, wv_hbm, wo_hbm, up_hbm, down_hbm)
    targets = (feats, wq, wk, msrc, mdst, mout, wv, wo, up, down)
    loads = [
        pltpu.make_async_copy(s, t, load_sem.at[i]) for i, (s, t) in enumerate(zip(sources, targets))
    ]
    for load in loads:
        load.start()

    me = lax.axis_index("dom")
    core = lax.rem(me, 2)
    chip = me // 2
    odd = lax.rem(chip, 2)
    pos = (1 - odd) * (chip // 2) + odd * (chips - 1 - chip // 2)

    def device_at(p):
        back = p // half
        return ((1 - back) * (2 * p) + back * (2 * (chips - 1 - p) + 1)) * 2 + core

    right = device_at(lax.rem(pos + 1, chips))
    left = device_at(lax.rem(pos + chips - 1, chips))
    pair = chip * 2 + 1 - core

    barrier = pltpu.get_barrier_semaphore()
    for k in range(1, n_dom):
        pl.semaphore_signal(barrier, inc=1, device_id={"dom": lax.rem(me + k, n_dom)}, device_id_type=MESH)

    lane = lax.broadcasted_iota(jnp.int32, (n_dom, lanes), 1)
    entries = jnp.zeros((n_dom, lanes), jnp.int32)
    lists = list_ref[0]
    for j in range(depth):
        entries = jnp.where(lane == me * depth + j, lists[:, j : j + 1], entries)
    for r in range(n_dom):
        list_out[r] = entries[r : r + 1, :]

    loads[0].wait()
    normed = rms_norm(feats[...], gain_ref[...]).astype(BF16)
    gathered[0, 0] = normed

    pl.semaphore_wait(barrier, n_dom - 1)

    def ring_copy(source, target, device):
        return pltpu.make_async_remote_copy(
            src_ref=gathered.at[source, 0],
            dst_ref=gathered.at[target, 0],
            send_sem=ring_send.at[target],
            recv_sem=ring_recv.at[target],
            device_id={"dom": device},
            device_id_type=MESH,
        )

    def half_copy(source, which, device):
        part = pl.ds(which * mid_row, mid_row)
        return pltpu.make_async_remote_copy(
            src_ref=gathered.at[source, 0, part],
            dst_ref=gathered.at[half, 0, part],
            send_sem=half_send.at[which],
            recv_sem=half_recv.at[which],
            device_id={"dom": device},
            device_id_type=MESH,
        )

    def pair_copy(slot):
        return pltpu.make_async_remote_copy(
            src_ref=gathered.at[slot, 0],
            dst_ref=gathered.at[slot, 1],
            send_sem=pair_send.at[slot],
            recv_sem=pair_recv.at[slot],
            device_id={"dom": pair},
            device_id_type=MESH,
        )

    def list_copy(k):
        to = lax.rem(me + k, n_dom)
        return pltpu.make_async_remote_copy(
            src_ref=list_out.at[to],
            dst_ref=list_in.at[k],
            send_sem=list_send.at[k],
            recv_sem=list_recv.at[k],
            device_id={"dom": to},
            device_id_type=MESH,
        )

    ring_copy(0, 1, right).start()
    ring_copy(0, chips - 1, left).start()
    pair_copy(0).start()
    for k in range(1, n_dom):
        list_copy(k).start()

    loads[1].wait()
    loads[2].wait()
    queries = dot(normed, wq[...]).astype(BF16)
    column = lax.broadcasted_iota(jnp.int32, (rows, width), 1)
    spread = jnp.concatenate(
        [jnp.where(column // head == h, queries, jnp.zeros_like(queries)) for h in range(HEADS)], axis=0
    )
    factor = head ** (-0.5) * math.log2(math.e)
    qk[...] = (dot(wk[...], spread, ((1,), (1,))) * factor).astype(BF16)

    span = qk.shape[1]
    step_columns = min(span, 2 * rows)

    def attend(block, first):
        for begin in range(0, span, step_columns):
            cols = pl.ds(begin, step_columns)
            scores = dot(block, qk[:, cols])
            block_top = jnp.max(scores, axis=0, keepdims=True)
            if first:
                new_top = block_top
            else:
                new_top = jnp.maximum(top[:, cols], block_top)
            weights = jnp.exp2(scores - new_top)
            sums = jnp.sum(weights, axis=0, keepdims=True)
            mixed = dot(block, weights.astype(BF16), ((0,), (0,)))
            if first:
                total[:, cols] = sums
                acc[:, cols] = mixed
            else:
                rescale = jnp.exp2(top[:, cols] - new_top)
                total[:, cols] = total[:, cols] * rescale + sums
                acc[:, cols] = acc[:, cols] * rescale + mixed
            top[:, cols] = new_top

    row_id = lax.broadcasted_iota(jnp.int32, (rows, lanes), 0)

    def pick(block, places):
        chosen = jnp.concatenate(
            [
                jnp.where(row_id + (offset * 2 + side) * rows == wanted_ref[...], 1.0, 0.0).astype(BF16)
                for offset, side in places
            ],
            axis=0,
        )
        return dot(chosen, block, ((0,), (0,)))

    def blocks_at(places):
        return jnp.concatenate([gathered[offset, side] for offset, side in places], axis=0)

    attend(normed, True)

    tiles, tile = src_ref.shape[1], src_ref.shape[2]
    source_rows = rows + lanes
    limit = limit_ref[0]
    slot_lane = lax.broadcasted_iota(jnp.int32, (n_dom, lanes), 1)
    slot_owner = lax.broadcasted_iota(jnp.int32, (n_dom, lanes), 0)
    counts = jnp.sum(
        jnp.where(slot_lane // depth == slot_owner, count_ref[...], 0), axis=0, keepdims=True
    )
    lane_row = lax.broadcasted_iota(jnp.int32, (1, lanes), 1)
    slot_live = jnp.where(
        (lax.rem(lane_row, depth) < counts) & (lane_row < slots), 1.0, 0.0
    ).astype(BF16)
    valid = jnp.broadcast_to(
        jnp.concatenate([jnp.ones((1, rows), BF16), slot_live], axis=1).astype(F32), (16, source_rows)
    ).astype(BF16)
    source_id = lax.broadcasted_iota(jnp.int32, (source_rows, tile), 0)
    node_id = lax.broadcasted_iota(jnp.int32, (rows, tile), 0)
    edge_lane = lax.broadcasted_iota(jnp.int32, (1, tile), 1)
    for t in range(tiles):
        cols = pl.ds(t * tile, tile)
        src = src_ref[0, t : t + 1, :]
        dst = dst_ref[0, t : t + 1, :]
        hot = jnp.where(source_id == src, 1.0, 0.0).astype(BF16)
        onehot_src[0:source_rows, cols] = hot
        onehot_src[source_rows : source_rows + rows, cols] = jnp.where(node_id == dst, 1.0, 0.0).astype(BF16)
        live = dot(valid, hot)[0:1, :]
        kept = jnp.where(edge_lane + t * tile < limit, live, 0.0)
        onehot_dst[:, cols] = jnp.where(node_id == dst, kept, 0.0).astype(BF16)

    for k in range(1, n_dom):
        list_copy(k).wait()
    asked = jnp.sum(jnp.where(slot_owner == me, entries, 0), axis=0, keepdims=True)
    for k in range(1, n_dom):
        asked = asked + list_in[k]
    owner = lane_row // depth
    owner_chip = owner // 2
    owner_odd = lax.rem(owner_chip, 2)
    owner_pos = (1 - owner_odd) * (owner_chip // 2) + owner_odd * (chips - 1 - owner_chip // 2)
    offset = pos - owner_pos
    offset = jnp.where(offset < 0, offset + chips, offset)
    side = jnp.where(lax.rem(owner, 2) == core, 0, 1)
    wanted_ref[...] = jnp.where(lane_row < slots, (offset * 2 + side) * rows + asked, -1)
    table[...] = pick(normed, [(0, 0)])

    def arrive(h):
        ring_copy(0, h, right).wait_recv()
        ring_copy(0, chips - h, left).wait_recv()

    def work(places):
        block = blocks_at(places)
        attend(block, False)
        table[...] += pick(block, places)

    def hop(h, last):
        ring_copy(0, h, right).wait_recv()
        if last:
            half_copy(h, 0, right).start()
        else:
            ring_copy(h, h + 1, right).start()
        pair_copy(h).start()
        ring_copy(0, chips - h, left).wait_recv()
        if last:
            half_copy(chips - h, 1, left).start()
        else:
            ring_copy(chips - h, chips - h - 1, left).start()
        pair_copy(chips - h).start()

    hop(1, half == 2)
    pair_copy(0).wait_recv()
    work([(1, 0), (chips - 1, 0), (0, 1)])

    def middle(h, last):
        hop(h, last)
        pair_copy(h - 1).wait_recv()
        pair_copy(chips - h + 1).wait_recv()
        work([(h, 0), (chips - h, 0), (h - 1, 1), (chips - h + 1, 1)])

    if half > 3:

        @pl.loop(2, half - 1)
        def _(h):
            middle(h, False)

    if half > 2:
        middle(half - 1, True)

    half_copy(0, 0, right).wait_recv()
    half_copy(0, 1, left).wait_recv()
    pair_copy(half).start()
    pair_copy(half - 1).wait_recv()
    pair_copy(half + 1).wait_recv()
    work([(half, 0), (half - 1, 1), (half + 1, 1)])
    for load in loads[3:]:
        load.wait()
    pair_copy(half).wait_recv()
    work([(half, 1)])

    own_source = dot(normed, msrc[...]).astype(BF16)
    far_source = dot(table[...].astype(BF16), msrc[...]).astype(BF16)
    own_dest = (dot(normed, mdst[...]) + msg_bias_ref[...]).astype(BF16)
    ends = jnp.concatenate([own_source, far_source, own_dest], axis=0)
    hidden = jax.nn.silu(dot(ends, onehot_src[...], ((0,), (0,)))).astype(BF16)
    chosen = onehot_dst[...]
    summed = dot(chosen, hidden, ((1,), (1,)))
    live_edges = jnp.sum(chosen.astype(F32), axis=1, keepdims=True)
    high = summed.astype(BF16)
    low = (summed - high.astype(F32)).astype(BF16)
    local_part = dot(high, mout[...]) + dot(low, mout[...]) + live_edges * msg_out_bias_ref[...]

    mixed = dot(wv[...], acc[...].astype(BF16), ((0,), (0,)))
    attended = jnp.concatenate(
        [
            mixed[h * head : (h + 1) * head, h * rows : (h + 1) * rows] / total[:, h * rows : (h + 1) * rows]
            for h in range(HEADS)
        ],
        axis=0,
    ).astype(BF16)
    mid = feats[...] + local_part + dot(attended, wo[...], ((0,), (0,)))
    mid_normed = rms_norm(mid, mlp_gain_ref[...]).astype(BF16)
    lifted = jax.nn.gelu(dot(mid_normed, up[...])).astype(BF16)
    out_ref[...] = mid + dot(lifted, down[...])

    for target in range(1, chips):
        if target != half:
            ring_copy(0, target, right).wait_send()
    for which in range(2):
        half_copy(0, which, right).wait_send()
    for slot in range(chips):
        pair_copy(slot).wait_send()


def body(
    node_feats,
    norm_gain,
    w_query,
    w_key,
    w_value,
    w_out,
    msg_src_w,
    msg_dst_w,
    msg_bias,
    msg_out_w,
    msg_out_bias,
    mlp_gain,
    mlp_up,
    mlp_down,
    send_list,
    send_count,
    edge_src,
    edge_dst,
    edge_count,
):
    rows, width = node_feats.shape
    n_dom = send_list.shape[1]
    chips = n_dom // 2
    slots = n_dom * send_list.shape[2]
    lanes = -(-slots // 128) * 128
    edges = edge_src.shape[1] * edge_src.shape[2]
    span = HEADS * rows
    large = (node_feats, w_query, w_key, msg_src_w, msg_dst_w, msg_out_w, w_value, w_out, mlp_up, mlp_down)
    vmem = pl.BlockSpec(memory_space=pltpu.VMEM)
    smem = pl.BlockSpec(memory_space=pltpu.SMEM)
    anywhere = pl.BlockSpec(memory_space=pl.ANY)
    dma = pltpu.SemaphoreType.DMA
    return pl.pallas_call(
        functools.partial(kernel, n_dom),
        out_shape=jax.ShapeDtypeStruct((rows, width), F32),
        in_specs=[vmem] * 8 + [smem] + [anywhere] * len(large),
        out_specs=vmem,
        scratch_shapes=[pltpu.VMEM(a.shape, a.dtype) for a in large]
        + [
            pltpu.VMEM((chips, 2, rows, width), BF16),
            pltpu.VMEM((n_dom, 1, lanes), jnp.int32),
            pltpu.VMEM((n_dom, 1, lanes), jnp.int32),
            pltpu.VMEM((1, lanes), jnp.int32),
            pltpu.VMEM((width, span), BF16),
            pltpu.VMEM((width, span), F32),
            pltpu.VMEM((1, span), F32),
            pltpu.VMEM((1, span), F32),
            pltpu.VMEM((lanes, width), F32),
            pltpu.VMEM((2 * rows + lanes, edges), BF16),
            pltpu.VMEM((rows, edges), BF16),
            dma((len(large),)),
            dma((chips,)),
            dma((chips,)),
            dma((2,)),
            dma((2,)),
            dma((chips,)),
            dma((chips,)),
            dma((n_dom,)),
            dma((n_dom,)),
        ],
        compiler_params=pltpu.CompilerParams(
            collective_id=0, has_side_effects=True, vmem_limit_bytes=40 * 1024 * 1024
        ),
    )(
        norm_gain.reshape(1, width),
        msg_bias.reshape(1, width),
        msg_out_bias.reshape(1, width),
        mlp_gain.reshape(1, width),
        send_list,
        send_count,
        edge_src,
        edge_dst,
        edge_count,
        *large,
    )


def solution(mesh):
    nodes = P(("graphs", "dom"), None)
    tiled = P(("graphs", "dom"), None, None)
    return jax.shard_map(
        body,
        mesh=mesh,
        in_specs=(nodes,) + (P(),) * 13 + (tiled, P("graphs", "dom"), tiled, tiled, P(("graphs", "dom"))),
        out_specs=nodes,
        check_vma=False,
    )
```

time: 94.9 us -> 39 us (0.41)
  waiting for transfers between devices: 28.6 us -> 0 us
  matrix products: 26.1 us -> 0 us
  Pallas kernels: 0 us -> 25.9 us
  between operations: 13.7 us -> 0.71 us
  starting transfers between devices: 7.39 us -> 0 us
  other arithmetic: 5.84 us -> 0 us
    dot_general x43 -> x0, matrix products: 26.1 us -> none  [the longest x8 6.79 us: tile_step(): jnp.dot(pick_src, slot_valid, preferred_element_type=jnp.float32) * in_range]
    pallas_call x0 -> x1, Pallas kernels: none -> 25.9 us  [body(): pl.pallas_call(functools.partial(kernel, n_dom), out_shape=jax.ShapeDtype...]
    all_gather x1 -> x0, waiting for transfers between devices: 24.5 us -> none  [body(): lax.all_gather(part, 'dom', axis=0, tiled=True)]
    unnamed x22 -> x39, local copies, waits for them, and re-layouts: 0.05 us -> 12 us
    all_to_all x1 -> x0, starting transfers between devices: 7.39 us -> none  [body(): lax.all_to_all(send_list[0], 'dom', split_axis=0, concat_axis=0, tiled=True)]
    eq x8 -> x0, local copies, waits for them, and re-layouts: 5.78 us -> none  [tile_step(): pick_src = (src_tile[:, None] == slot_ids[None, :]).astype(jnp.bfloat16)]
    all_to_all x1 -> x0, waiting for transfers between devices: 4.12 us -> none  [body(): lax.all_to_all(send_list[0], 'dom', split_axis=0, concat_axis=0, tiled=True)]
    reduce_sum x3 -> x0, other arithmetic: 2.45 us -> none  [the longest x2 1.39 us: attend_block(): new_total = run_total * rescale + jnp.sum(weights, axis=-1)]
  transfers between devices with their start and end apart: 2 -> 0, of which waited for: 2 -> 0; matrix products, arithmetic and copies ran while one was open for 5% -> 0% of each run, Pallas kernels for 0% -> 0%
where the time goes in v1:
time: 39 us; the launch traced here: 38.6 us
  Pallas kernels  25.9 us (66%)
  local copies, waits for them, and re-layouts  12 us (31%)
  between operations  0.71 us (2%)
    pallas_call x1, Pallas kernels, body(): pl.pallas_call(functools.partial(kernel, n_dom), out_shape=jax.ShapeDtype...  25.9 us
    unnamed x39, local copies, waits for them, and re-layouts  12 us

profile of v1, /device:TPU:0, one launch (start us, length us, event | category | flops | bytes accessed | tf_op | source)
XLA Modules:
  0.0 38.6 jit_solution(7565772205939376109)
XLA Ops:
  0.7 0.0 copy-start.16
  0.7 0.7 %copy-done.16 = s32[1,16,4]{1,2,0:T(4,128)S(1)} copy-done((s32[1,16,4]{1,2,0:T(4,128)S(1)}, s32[1,16,4]{1,2,0:T(4,128)}, u32[]{:S(2)}) %copy-start.16) | copy-done | bytes 280
  1.3 0.0 copy-start.15
  1.4 0.1 copy.20.list_ref
  1.4 0.6 %copy-done.17 = s32[16,1]{0,1:T(1,128)S(1)} copy-done((s32[16,1]{0,1:T(1,128)S(1)}, s32[16,1]{0,1:T(1,128)}, u32[]{:S(2)}) %copy-start.17) | copy-done | bytes 88
  2.0 0.1 copy.21.count_ref
  2.1 0.0 copy-done.12
  2.1 0.0 copy-done.13
  2.1 0.0 copy-done.14
  2.1 0.0 copy-done.15
  2.1 0.6 %copy-done.10 = s32[1,8,128]{2,1,0:T(8,128)S(1)} copy-done((s32[1,8,128]{2,1,0:T(8,128)S(1)}, s32[1,8,128]{2,1,0:T(8,128)}, u32[]{:S(2)}) %copy-start.10) | copy-done | bytes 4120
  2.7 0.0 copy-done.11
  2.7 1.0 %copy-done = bf16[256,1024]{1,0:T(8,128)(2,1)S(1)} copy-done((bf16[256,1024]{1,0:T(8,128)(2,1)S(1)}, bf16[256,1024]{1,0:T(8,128)(2,1)}, u32[]{:S(2)}) %copy-start) | copy-done | bytes 524312
  3.7 1.0 %copy-done.1 = bf16[1024,256]{1,0:T(8,128)(2,1)S(1)} copy-done((bf16[1024,256]{1,0:T(8,128)(2,1)S(1)}, bf16[1024,256]{1,0:T(8,128)(2,1)}, u32[]{:S(2)}) %copy-start.1) | copy-done | bytes 524312
  4.8 0.9 %copy-done.2 = f32[128,256]{1,0:T(8,128)S(1)} copy-done((f32[128,256]{1,0:T(8,128)S(1)}, f32[128,256]{1,0:T(8,128)}, u32[]{:S(2)}) %copy-start.2) | copy-done | bytes 131096
  5.7 0.9 %copy-done.3 = bf16[256,256]{1,0:T(8,128)(2,1)S(1)} copy-done((bf16[256,256]{1,0:T(8,128)(2,1)S(1)}, bf16[256,256]{1,0:T(8,128)(2,1)}, u32[]{:S(2)}) %copy-start.3) | copy-done | bytes 131096
  6.6 0.9 %copy-done.4 = bf16[256,256]{1,0:T(8,128)(2,1)S(1)} copy-done((bf16[256,256]{1,0:T(8,128)(2,1)S(1)}, bf16[256,256]{1,0:T(8,128)(2,1)}, u32[]{:S(2)}) %copy-start.4) | copy-done | bytes 131096
  7.5 0.9 %copy-done.5 = bf16[256,256]{1,0:T(8,128)(2,1)S(1)} copy-done((bf16[256,256]{1,0:T(8,128)(2,1)S(1)}, bf16[256,256]{1,0:T(8,128)(2,1)}, u32[]{:S(2)}) %copy-start.5) | copy-done | bytes 131096
  8.4 0.9 %copy-done.6 = bf16[256,256]{1,0:T(8,128)(2,1)S(1)} copy-done((bf16[256,256]{1,0:T(8,128)(2,1)S(1)}, bf16[256,256]{1,0:T(8,128)(2,1)}, u32[]{:S(2)}) %copy-start.6) | copy-done | bytes 131096
  9.3 0.9 %copy-done.7 = bf16[256,256]{1,0:T(8,128)(2,1)S(1)} copy-done((bf16[256,256]{1,0:T(8,128)(2,1)S(1)}, bf16[256,256]{1,0:T(8,128)(2,1)}, u32[]{:S(2)}) %copy-start.7) | copy-done | bytes 131096
  10.2 0.9 %copy-done.8 = bf16[256,256]{1,0:T(8,128)(2,1)S(1)} copy-done((bf16[256,256]{1,0:T(8,128)(2,1)S(1)}, bf16[256,256]{1,0:T(8,128)(2,1)}, u32[]{:S(2)}) %copy-start.8) | copy-done | bytes 131096
  11.1 0.9 %copy-done.9 = bf16[256,256]{1,0:T(8,128)(2,1)S(1)} copy-done((bf16[256,256]{1,0:T(8,128)(2,1)S(1)}, bf16[256,256]{1,0:T(8,128)(2,1)}, u32[]{:S(2)}) %copy-start.9) | copy-done | bytes 131096
  12.0 25.9 %shard_map.181 = f32[128,256]{1,0:T(8,128)S(1)} custom-call(f32[1,256]{1,0:T(1,128)S(1)} %bitcast.4, f32[1,256]{1,0:T(1,128)S(1)} %bitcast.5, f32[1,256]{1,0:T(1,128)S(1)} %bitcast.6, f32[1,256]{1,0:T(1,128)S(1)} %bitcast.7, s32[1,16,4]{2,1,0:T(8,128)S(1)} %copy.20.list_ref, s32[16,1]{1,0:T(8,128)S(1)} %copy.21.count_ref, s32[1,8,128]{2,1,0:T(8,128)S(1)} %copy-done.10, ...), custom_call_target="tpu_custom_call" | custom-call | tf_op jit(solution)/shard_map/pallas_call | solution.py:390
  38.0 0.7 %copy.24 = f32[128,256]{1,0:T(8,128)} copy(f32[128,256]{1,0:T(8,128)S(1)} %shard_map.181) | data formatting | bytes 262144
  (16 shorter events, 0.0 us)
Async XLA Ops:
  0.7 0.7 %copy-start.16 = (s32[1,16,4]{1,2,0:T(4,128)S(1)}, s32[1,16,4]{1,2,0:T(4,128)}, u32[]{:S(2)}) copy-start(s32[1,16,4]{1,2,0:T(4,128)} %param.33) | copy-start | bytes 772
  1.3 0.7 %copy-start.17 = (s32[16,1]{0,1:T(1,128)S(1)}, s32[16,1]{0,1:T(1,128)}, u32[]{:S(2)}) copy-start(s32[16,1]{0,1:T(1,128)} %param.34) | copy-start | bytes 196
  1.3 0.7 %copy-start.12 = (f32[256]{0:T(256)S(1)}, f32[256]{0:T(256)}, u32[]{:S(2)}) copy-start(f32[256]{0:T(256)} %param.20) | copy-start | bytes 3076
  1.3 0.7 %copy-start.13 = (f32[256]{0:T(256)S(1)}, f32[256]{0:T(256)}, u32[]{:S(2)}) copy-start(f32[256]{0:T(256)} %param.27) | copy-start | bytes 3076
  1.3 0.7 %copy-start.14 = (f32[256]{0:T(256)S(1)}, f32[256]{0:T(256)}, u32[]{:S(2)}) copy-start(f32[256]{0:T(256)} %param.29) | copy-start | bytes 3076
  1.3 0.7 %copy-start.15 = (f32[256]{0:T(256)S(1)}, f32[256]{0:T(256)}, u32[]{:S(2)}) copy-start(f32[256]{0:T(256)} %param.30) | copy-start | bytes 3076
  2.0 0.7 %copy-start.10 = (s32[1,8,128]{2,1,0:T(8,128)S(1)}, s32[1,8,128]{2,1,0:T(8,128)}, u32[]{:S(2)}) copy-start(s32[1,8,128]{2,1,0:T(8,128)} %src_ref.1) | copy-start | bytes 12292
  2.0 0.7 %copy-start.11 = (s32[1,8,128]{2,1,0:T(8,128)S(1)}, s32[1,8,128]{2,1,0:T(8,128)}, u32[]{:S(2)}) copy-start(s32[1,8,128]{2,1,0:T(8,128)} %dst_ref.1) | copy-start | bytes 12292
  2.7 1.0 %copy-start = (bf16[256,1024]{1,0:T(8,128)(2,1)S(1)}, bf16[256,1024]{1,0:T(8,128)(2,1)}, u32[]{:S(2)}) copy-start(bf16[256,1024]{1,0:T(8,128)(2,1)} %up_hbm.1) | copy-start | bytes 1572868
  3.7 1.0 %copy-start.1 = (bf16[1024,256]{1,0:T(8,128)(2,1)S(1)}, bf16[1024,256]{1,0:T(8,128)(2,1)}, u32[]{:S(2)}) copy-start(bf16[1024,256]{1,0:T(8,128)(2,1)} %down_hbm.1) | copy-start | bytes 1572868
  4.8 0.9 %copy-start.2 = (f32[128,256]{1,0:T(8,128)S(1)}, f32[128,256]{1,0:T(8,128)}, u32[]{:S(2)}) copy-start(f32[128,256]{1,0:T(8,128)} %feats_hbm.1) | copy-start | bytes 393220
  5.7 0.9 %copy-start.3 = (bf16[256,256]{1,0:T(8,128)(2,1)S(1)}, bf16[256,256]{1,0:T(8,128)(2,1)}, u32[]{:S(2)}) copy-start(bf16[256,256]{1,0:T(8,128)(2,1)} %wq_hbm.1) | copy-start | bytes 393220
  6.6 0.9 %copy-start.4 = (bf16[256,256]{1,0:T(8,128)(2,1)S(1)}, bf16[256,256]{1,0:T(8,128)(2,1)}, u32[]{:S(2)}) copy-start(bf16[256,256]{1,0:T(8,128)(2,1)} %wk_hbm.1) | copy-start | bytes 393220
  7.5 0.9 %copy-start.5 = (bf16[256,256]{1,0:T(8,128)(2,1)S(1)}, bf16[256,256]{1,0:T(8,128)(2,1)}, u32[]{:S(2)}) copy-start(bf16[256,256]{1,0:T(8,128)(2,1)} %msrc_hbm.1) | copy-start | bytes 393220
  8.4 0.9 %copy-start.6 = (bf16[256,256]{1,0:T(8,128)(2,1)S(1)}, bf16[256,256]{1,0:T(8,128)(2,1)}, u32[]{:S(2)}) copy-start(bf16[256,256]{1,0:T(8,128)(2,1)} %mdst_hbm.1) | copy-start | bytes 393220
  9.3 0.9 %copy-start.7 = (bf16[256,256]{1,0:T(8,128)(2,1)S(1)}, bf16[256,256]{1,0:T(8,128)(2,1)}, u32[]{:S(2)}) copy-start(bf16[256,256]{1,0:T(8,128)(2,1)} %mout_hbm.1) | copy-start | bytes 393220
  10.2 0.9 %copy-start.8 = (bf16[256,256]{1,0:T(8,128)(2,1)S(1)}, bf16[256,256]{1,0:T(8,128)(2,1)}, u32[]{:S(2)}) copy-start(bf16[256,256]{1,0:T(8,128)(2,1)} %wv_hbm.1) | copy-start | bytes 393220
  11.1 0.9 %copy-start.9 = (bf16[256,256]{1,0:T(8,128)(2,1)S(1)}, bf16[256,256]{1,0:T(8,128)(2,1)}, u32[]{:S(2)}) copy-start(bf16[256,256]{1,0:T(8,128)(2,1)} %wo_hbm.1) | copy-start | bytes 393220

commit v2 on v1

--- a/solution.py
+++ b/solution.py
@@ -18,42 +18,30 @@
     return lax.dot_general(a, b, (dims, ((), ())), preferred_element_type=F32)
 
 
+def exact_dot(a, b, dims=((1,), (0,))):
+    return lax.dot_general(
+        a, b, (dims, ((), ())), preferred_element_type=F32, precision=lax.Precision.HIGHEST
+    )
+
+
 def rms_norm(features, gain):
     return features * lax.rsqrt(jnp.mean(features * features, axis=-1, keepdims=True) + 1e-06) * gain
 
 
 def kernel(
     n_dom,
-    gain_ref,
-    msg_bias_ref,
-    msg_out_bias_ref,
-    mlp_gain_ref,
-    list_ref,
-    count_ref,
-    src_ref,
-    dst_ref,
-    limit_ref,
-    feats_hbm,
-    wq_hbm,
-    wk_hbm,
-    msrc_hbm,
-    mdst_hbm,
-    mout_hbm,
-    wv_hbm,
-    wo_hbm,
-    up_hbm,
-    down_hbm,
+    count,
+    *refs,
+):
+    sources, out_ref, targets = refs[:count], refs[count], refs[count + 1 : 2 * count + 1]
+    run(n_dom, sources, out_ref, targets, *refs[2 * count + 1 :])
+
+
+def run(
+    n_dom,
+    sources,
     out_ref,
-    feats,
-    wq,
-    wk,
-    msrc,
-    mdst,
-    mout,
-    wv,
-    wo,
-    up,
-    down,
+    targets,
     gathered,
     list_out,
     list_in,
@@ -75,8 +63,29 @@
     list_send,
     list_recv,
 ):
+    (
+        feats,
+        gain_ref,
+        list_ref,
+        wq,
+        wk,
+        count_ref,
+        src_ref,
+        dst_ref,
+        limit_ref,
+        msrc,
+        mdst,
+        msg_bias_ref,
+        mout,
+        msg_out_bias_ref,
+        wv,
+        wo,
+        mlp_gain_ref,
+        up,
+        down,
+    ) = targets
     rows, width = feats.shape
-    depth = list_ref.shape[-1]
+    depth = list_ref.shape[1]
     slots = n_dom * depth
     lanes = table.shape[0]
     chips = n_dom // 2
@@ -84,8 +93,6 @@
     mid_row = rows // 2
     head = width // HEADS
 
-    sources = (feats_hbm, wq_hbm, wk_hbm, msrc_hbm, mdst_hbm, mout_hbm, wv_hbm, wo_hbm, up_hbm, down_hbm)
-    targets = (feats, wq, wk, msrc, mdst, mout, wv, wo, up, down)
     loads = [
         pltpu.make_async_copy(s, t, load_sem.at[i]) for i, (s, t) in enumerate(zip(sources, targets))
     ]
@@ -110,17 +117,18 @@
     for k in range(1, n_dom):
         pl.semaphore_signal(barrier, inc=1, device_id={"dom": lax.rem(me + k, n_dom)}, device_id_type=MESH)
 
-    lane = lax.broadcasted_iota(jnp.int32, (n_dom, lanes), 1)
-    entries = jnp.zeros((n_dom, lanes), jnp.int32)
-    lists = list_ref[0]
-    for j in range(depth):
-        entries = jnp.where(lane == me * depth + j, lists[:, j : j + 1], entries)
+    loads[0].wait()
+    loads[1].wait()
+    normed = rms_norm(feats[...], gain_ref[...]).astype(BF16)
+    gathered[0, 0] = normed
+    loads[2].wait()
+    place = lax.broadcasted_iota(jnp.int32, (depth, lanes), 1) - me * depth
+    place = place == lax.broadcasted_iota(jnp.int32, (depth, lanes), 0)
+    entries = exact_dot(
+        list_ref[0].astype(F32), jnp.where(place, 1.0, 0.0), ((0,), (0,))
+    ).astype(jnp.int32)
     for r in range(n_dom):
         list_out[r] = entries[r : r + 1, :]
-
-    loads[0].wait()
-    normed = rms_norm(feats[...], gain_ref[...]).astype(BF16)
-    gathered[0, 0] = normed
 
     pl.semaphore_wait(barrier, n_dom - 1)
 
@@ -172,8 +180,8 @@
     for k in range(1, n_dom):
         list_copy(k).start()
 
-    loads[1].wait()
-    loads[2].wait()
+    loads[3].wait()
+    loads[4].wait()
     queries = dot(normed, wq[...]).astype(BF16)
     column = lax.broadcasted_iota(jnp.int32, (rows, width), 1)
     spread = jnp.concatenate(
@@ -186,6 +194,7 @@
     step_columns = min(span, 2 * rows)
 
     def attend(block, first):
+        turned = jnp.transpose(block)
         for begin in range(0, span, step_columns):
             cols = pl.ds(begin, step_columns)
             scores = dot(block, qk[:, cols])
@@ -196,7 +205,7 @@
                 new_top = jnp.maximum(top[:, cols], block_top)
             weights = jnp.exp2(scores - new_top)
             sums = jnp.sum(weights, axis=0, keepdims=True)
-            mixed = dot(block, weights.astype(BF16), ((0,), (0,)))
+            mixed = dot(turned, weights.astype(BF16))
             if first:
                 total[:, cols] = sums
                 acc[:, cols] = mixed
@@ -222,15 +231,18 @@
         return jnp.concatenate([gathered[offset, side] for offset, side in places], axis=0)
 
     attend(normed, True)
+    for load in loads[5:9]:
+        load.wait()
 
     tiles, tile = src_ref.shape[1], src_ref.shape[2]
     source_rows = rows + lanes
-    limit = limit_ref[0]
+    limit = limit_ref[...]
     slot_lane = lax.broadcasted_iota(jnp.int32, (n_dom, lanes), 1)
     slot_owner = lax.broadcasted_iota(jnp.int32, (n_dom, lanes), 0)
-    counts = jnp.sum(
-        jnp.where(slot_lane // depth == slot_owner, count_ref[...], 0), axis=0, keepdims=True
-    )
+    counts = exact_dot(
+        jnp.broadcast_to(count_ref[...], (8, n_dom)).astype(F32),
+        jnp.where(slot_lane // depth == slot_owner, 1.0, 0.0),
+    )[0:1, :].astype(jnp.int32)
     lane_row = lax.broadcasted_iota(jnp.int32, (1, lanes), 1)
     slot_live = jnp.where(
         (lax.rem(lane_row, depth) < counts) & (lane_row < slots), 1.0, 0.0
@@ -267,10 +279,6 @@
     wanted_ref[...] = jnp.where(lane_row < slots, (offset * 2 + side) * rows + asked, -1)
     table[...] = pick(normed, [(0, 0)])
 
-    def arrive(h):
-        ring_copy(0, h, right).wait_recv()
-        ring_copy(0, chips - h, left).wait_recv()
-
     def work(places):
         block = blocks_at(places)
         attend(block, False)
@@ -315,7 +323,7 @@
     pair_copy(half - 1).wait_recv()
     pair_copy(half + 1).wait_recv()
     work([(half, 0), (half - 1, 1), (half + 1, 1)])
-    for load in loads[3:]:
+    for load in loads[9:]:
         load.wait()
     pair_copy(half).wait_recv()
     work([(half, 1)])
@@ -382,54 +390,61 @@
     lanes = -(-slots // 128) * 128
     edges = edge_src.shape[1] * edge_src.shape[2]
     span = HEADS * rows
-    large = (node_feats, w_query, w_key, msg_src_w, msg_dst_w, msg_out_w, w_value, w_out, mlp_up, mlp_down)
-    vmem = pl.BlockSpec(memory_space=pltpu.VMEM)
-    smem = pl.BlockSpec(memory_space=pltpu.SMEM)
-    anywhere = pl.BlockSpec(memory_space=pl.ANY)
-    dma = pltpu.SemaphoreType.DMA
-    return pl.pallas_call(
-        functools.partial(kernel, n_dom),
-        out_shape=jax.ShapeDtypeStruct((rows, width), F32),
-        in_specs=[vmem] * 8 + [smem] + [anywhere] * len(large),
-        out_specs=vmem,
-        scratch_shapes=[pltpu.VMEM(a.shape, a.dtype) for a in large]
-        + [
-            pltpu.VMEM((chips, 2, rows, width), BF16),
-            pltpu.VMEM((n_dom, 1, lanes), jnp.int32),
-            pltpu.VMEM((n_dom, 1, lanes), jnp.int32),
-            pltpu.VMEM((1, lanes), jnp.int32),
-            pltpu.VMEM((width, span), BF16),
-            pltpu.VMEM((width, span), F32),
-            pltpu.VMEM((1, span), F32),
-            pltpu.VMEM((1, span), F32),
-            pltpu.VMEM((lanes, width), F32),
-            pltpu.VMEM((2 * rows + lanes, edges), BF16),
-            pltpu.VMEM((rows, edges), BF16),
-            dma((len(large),)),
-            dma((chips,)),
-            dma((chips,)),
-            dma((2,)),
-            dma((2,)),
-            dma((chips,)),
-            dma((chips,)),
-            dma((n_dom,)),
-            dma((n_dom,)),
-        ],
-        compiler_params=pltpu.CompilerParams(
-            collective_id=0, has_side_effects=True, vmem_limit_bytes=40 * 1024 * 1024
-        ),
-    )(
-        norm_gain.reshape(1, width),
-        msg_bias.reshape(1, width),
-        msg_out_bias.reshape(1, width),
-        mlp_gain.reshape(1, width),
-        send_list,
-        send_count,
+    line = lambda vector: vector.reshape(1, -1)
+    operands = (
+        node_feats,
+        line(norm_gain),
+        jnp.transpose(send_list, (0, 2, 1)),
+        w_query,
+        w_key,
+        jnp.transpose(send_count),
         edge_src,
         edge_dst,
-        edge_count,
-        *large,
+        line(edge_count),
+        msg_src_w,
+        msg_dst_w,
+        line(msg_bias),
+        msg_out_w,
+        line(msg_out_bias),
+        w_value,
+        w_out,
+        line(mlp_gain),
+        mlp_up,
+        mlp_down,
     )
+    dma = pltpu.SemaphoreType.DMA
+    scratch = [
+        pltpu.VMEM((chips, 2, rows, width), BF16),
+        pltpu.VMEM((n_dom, 1, lanes), jnp.int32),
+        pltpu.VMEM((n_dom, 1, lanes), jnp.int32),
+        pltpu.VMEM((1, lanes), jnp.int32),
+        pltpu.VMEM((width, span), BF16),
+        pltpu.VMEM((width, span), F32),
+        pltpu.VMEM((1, span), F32),
+        pltpu.VMEM((1, span), F32),
+        pltpu.VMEM((lanes, width), F32),
+        pltpu.VMEM((2 * rows + lanes, edges), BF16),
+        pltpu.VMEM((rows, edges), BF16),
+        dma((len(operands),)),
+        dma((chips,)),
+        dma((chips,)),
+        dma((2,)),
+        dma((2,)),
+        dma((chips,)),
+        dma((chips,)),
+        dma((n_dom,)),
+        dma((n_dom,)),
+    ]
+    return pl.pallas_call(
+        functools.partial(kernel, n_dom, len(operands)),
+        out_shape=jax.ShapeDtypeStruct((rows, width), F32),
+        in_specs=[pl.BlockSpec(memory_space=pltpu.HBM)] * len(operands),
+        out_specs=pl.BlockSpec(memory_space=pltpu.VMEM),
+        scratch_shapes=[pltpu.VMEM(a.shape, a.dtype) for a in operands] + scratch,
+        compiler_params=pltpu.CompilerParams(
+            collective_id=0, has_side_effects=True, vmem_limit_bytes=64 * 1024 * 1024 - 65536
+        ),
+    )(*operands)
 
 
 def solution(mesh):

time: 39 us -> 27.7 us (0.71)
  local copies, waits for them, and re-layouts: 12 us -> 1.57 us
  Pallas kernels: 25.9 us -> 25.3 us
    unnamed x39 -> x1, local copies, waits for them, and re-layouts: 12 us -> 1.57 us
    pallas_call x1, Pallas kernels: 25.9 us -> 25.3 us  [body(): pl.pallas_call(functools.partial(kernel, n_dom, len(operands)), out_shape...]
where the time goes in v2:
time: 27.7 us; the launch traced here: 27.5 us
  Pallas kernels  25.3 us (91%)
  local copies, waits for them, and re-layouts  1.57 us (6%)
  between operations  0.66 us (2%)
    pallas_call x1, Pallas kernels, body(): pl.pallas_call(functools.partial(kernel, n_dom, len(operands)), out_shape...  25.3 us
    unnamed x1, local copies, waits for them, and re-layouts  1.57 us

profile of v2, /device:TPU:0, one launch (start us, length us, event | category | flops | bytes accessed | tf_op | source)
XLA Modules:
  0.0 27.5 jit_solution(9456048702491743774)
XLA Ops:
  0.7 25.3 %shard_map.181 = f32[128,256]{1,0:T(8,128)} custom-call(f32[128,256]{1,0:T(8,128)} %refs_0_.1, f32[1,256]{1,0:T(1,128)} %bitcast.9, s32[1,4,16]{2,1,0:T(4,128)} %bitcast.8, bf16[256,256]{1,0:T(8,128)(2,1)} %refs_3_.1, bf16[256,256]{1,0:T(8,128)(2,1)} %refs_4_.1, s32[1,16]{1,0:T(1,128)} %bitcast.13, s32[1,8,128]{2,1,0:T(8,128)} %refs_6_.1, ...), custom_call_target="tpu_custom_call" | custom-call | tf_op jit(solution)/shard_map/pallas_call | solution.py:438
  26.0 1.6 %copy.22 = f32[128,256]{1,0:T(8,128)} copy(f32[128,256]{1,0:T(8,128)} %shard_map.181) | data formatting | bytes 262144
